TPU v7x, 32 devices: a whole 2x2x4 slice. The times are simulated.
32 devices in a mesh: group: 2 (over x), tile: 8 (over z, y), draw: 2 (over core).
Axes of the slice: x: 2, y: 2, z: 4, core: 2. Of those that a mesh axis runs over, the one named last changes fastest.
Arguments:
- inputs: bfloat16 [4, 32, 270, 256], P(('group', 'draw'), 'tile'), parts along dimension 0, may hold values from -6 to 6
- land_mask: int32 [32, 270], P('tile'), may hold values 0 or 1
- kernel: float32 [7, 7, 256], replicated, may hold values from -0.875 to 0.875
- conv_bias: float32 [256], replicated, may hold values from -3 to 3
- norm_gain: float32 [256], replicated, may hold values from 0.1 to 1.9
- norm_bias: float32 [256], replicated, may hold values from -3 to 3
- w_in: bfloat16 [256, 1024], replicated, may hold values from -0.375 to 0.375
- b_in: float32 [1024], replicated, may hold values from -3 to 3
- w_out: bfloat16 [1024, 256], replicated, may hold values from -0.1875 to 0.1875
- b_out: float32 [256], replicated, may hold values from -3 to 3
- layer_scale: float32 [256], replicated, may hold values from 0.1 to 1.9
- cotangent: bfloat16 [4, 32, 270, 256], P(('group', 'draw'), 'tile'), parts along dimension 0, may hold values from -6 to 6
Outputs:
- output: bfloat16 [4, 32, 270, 256], P(('group', 'draw'), 'tile'), parts along dimension 0
- input_grad: bfloat16 [4, 32, 270, 256], P(('group', 'draw'), 'tile'), parts along dimension 0
- kernel_grad: float32 [14, 7, 256], P('group'), parts along dimension 0
- w_in_grad: float32 [512, 1024], P('group'), parts along dimension 0
- w_out_grad: float32 [2048, 256], P('group'), parts along dimension 0
- b_in_grad: float32 [2048], P('group'), parts along dimension 0
- channel_grads: float32 [10, 256], P('group'), parts along dimension 0
There are 2 independent parts, one for each index of `group`. A program takes and returns all parts, laid end to end along the dimension named above; an argument that names none is the same for every part. Nothing has to cross between parts.
All inputs are finite; a program needn't handle non-finite values. No bound on the sum of `land_mask` on one device may be relied on, other than what follows from the above.
Results may differ from a plain program's by a relative error of at most 0.007.
Values may be sent and summed in bfloat16 or wider, within the bound.
A program may use at most 64 MiB of HBM per device.

v0:
```python
import jax
import jax.numpy as jnp
from jax import lax
from jax.sharding import PartitionSpec as P

ROOT_TERM = 0.7978845608028654
CUBIC = 0.044715
EPSILON = 1e-06


def with_halo(cells, sides, width):
    for axis, dim in sides:
        count = lax.axis_size(axis)
        ends = count - 1
        head = lax.slice_in_dim(cells, 0, width, axis=dim)
        tail = lax.slice_in_dim(cells, cells.shape[dim] - width, cells.shape[dim], axis=dim)
        cells = jnp.concatenate(
            [
                lax.ppermute(tail, axis, [(i, (i + 1) % count) for i in range(ends)]),
                cells,
                lax.ppermute(head, axis, [((i + 1) % count, i) for i in range(ends)]),
            ],
            axis=dim,
        )
    return cells


def lon_wrap(values):
    return jnp.concatenate([values[:, :, -3:], values, values[:, :, :3]], axis=2)


def apply_taps(padded, weights, height, breadth):
    total = jnp.zeros((padded.shape[0], height, breadth, padded.shape[3]), jnp.float32)
    for row_off in range(7):
        for col_off in range(7):
            total = (
                total
                + padded[:, row_off : row_off + height, col_off : col_off + breadth, :]
                * weights[row_off, col_off]
            )
    return total


def kernel_terms(padded, grad_map, height, breadth):
    rows_list = []
    for row_off in range(7):
        cells_list = []
        for col_off in range(7):
            window = padded[:, row_off : row_off + height, col_off : col_off + breadth, :]
            cells_list.append(jnp.sum(window * grad_map, axis=(0, 1, 2)))
        rows_list.append(jnp.stack(cells_list))
    return jnp.stack(rows_list)


def gelu_slope(hidden):
    inner = ROOT_TERM * (hidden + CUBIC * hidden * hidden * hidden)
    tanh_value = jnp.tanh(inner)
    return 0.5 * (1.0 + tanh_value) + 0.5 * hidden * (1.0 - tanh_value * tanh_value) * ROOT_TERM * (
        1.0 + 3.0 * CUBIC * hidden * hidden
    )


def grad_extend(values):
    return with_halo(values, (("tile", 1),), 3)


def per_device(
    inputs,
    land_mask,
    kernel,
    conv_bias,
    norm_gain,
    norm_bias,
    w_in,
    b_in,
    w_out,
    b_out,
    layer_scale,
    cotangent,
):
    height = inputs.shape[1]
    breadth = inputs.shape[2]
    channels = inputs.shape[3]
    padded_state = with_halo(inputs, (("tile", 1),), 3)
    wrapped = lon_wrap(padded_state.astype(jnp.float32))
    conv_out = apply_taps(wrapped, kernel, height, breadth) + conv_bias
    center = jnp.mean(conv_out, axis=-1, keepdims=True)
    deviation = conv_out - center
    inv_std = lax.rsqrt(jnp.mean(deviation * deviation, axis=-1, keepdims=True) + EPSILON)
    unit = deviation * inv_std
    normed = (unit * norm_gain + norm_bias).astype(jnp.bfloat16).reshape(-1, channels)
    hidden = jnp.dot(normed, w_in, preferred_element_type=jnp.float32) + b_in
    inner = ROOT_TERM * (hidden + CUBIC * hidden * hidden * hidden)
    activated = (0.5 * hidden * (1.0 + jnp.tanh(inner))).astype(jnp.bfloat16)
    mixed = (jnp.dot(activated, w_out, preferred_element_type=jnp.float32) + b_out).reshape(
        inputs.shape
    )
    ocean = land_mask.astype(jnp.float32)[None, :, :, None]
    output = (inputs.astype(jnp.float32) + ocean * layer_scale * mixed).astype(jnp.bfloat16)
    upstream = cotangent.astype(jnp.float32)
    scale_part = jnp.sum(ocean * upstream * mixed, axis=(0, 1, 2))
    grad_mixed = (ocean * layer_scale * upstream).astype(jnp.bfloat16).reshape(-1, channels)
    out_bias_part = jnp.sum(grad_mixed.astype(jnp.float32), axis=0)
    w_out_part = lax.dot_general(
        activated, grad_mixed, (((0,), (0,)), ((), ())), preferred_element_type=jnp.float32
    )
    grad_act = lax.dot_general(
        grad_mixed, w_out, (((1,), (1,)), ((), ())), preferred_element_type=jnp.float32
    )
    grad_hidden = (grad_act * gelu_slope(hidden)).astype(jnp.bfloat16)
    w_in_part = lax.dot_general(
        normed, grad_hidden, (((0,), (0,)), ((), ())), preferred_element_type=jnp.float32
    )
    hidden_bias_part = jnp.sum(grad_hidden.astype(jnp.float32), axis=0)
    grad_normed = lax.dot_general(
        grad_hidden, w_in, (((1,), (1,)), ((), ())), preferred_element_type=jnp.float32
    ).reshape(inputs.shape)
    gain_part = jnp.sum(grad_normed * unit, axis=(0, 1, 2))
    nbias_part = jnp.sum(grad_normed, axis=(0, 1, 2))
    scaled = grad_normed * norm_gain
    grad_conv = (
        inv_std
        * (
            scaled
            - jnp.mean(scaled, axis=-1, keepdims=True)
            - unit * jnp.mean(scaled * unit, axis=-1, keepdims=True)
        )
    ).astype(jnp.bfloat16)
    grad_float = grad_conv.astype(jnp.float32)
    conv_bias_part = jnp.sum(grad_float, axis=(0, 1, 2))
    kernel_part = kernel_terms(wrapped, grad_float, height, breadth)
    grad_padded = lon_wrap(grad_extend(grad_conv).astype(jnp.float32))
    input_grad = (upstream + apply_taps(grad_padded, kernel[::-1, ::-1], height, breadth)).astype(
        jnp.bfloat16
    )
    channel_part = jnp.stack([conv_bias_part, gain_part, nbias_part, out_bias_part, scale_part])
    kernel_sum, w_in_sum, w_out_sum, hidden_sum, channel_sum = lax.psum(
        (kernel_part, w_in_part, w_out_part, hidden_bias_part, channel_part), ("tile", "draw")
    )
    total_cells = inputs.shape[0] * lax.axis_size("draw") * height * lax.axis_size("tile") * breadth
    factor = 1.0 / jnp.sqrt(jnp.float32(total_cells))
    return (
        output,
        input_grad,
        kernel_sum * factor,
        w_in_sum * factor,
        w_out_sum * factor,
        hidden_sum * factor,
        channel_sum * factor,
    )


def solution(mesh):
    placed = (
        P(("group", "draw"), "tile", None, None),
        P("tile", None),
        P(),
        P(),
        P(),
        P(),
        P(),
        P(),
        P(),
        P(),
        P(),
        P(("group", "draw"), "tile", None, None),
    )
    return jax.shard_map(
        per_device,
        mesh=mesh,
        in_specs=placed,
        out_specs=(
            P(("group", "draw"), "tile", None, None),
            P(("group", "draw"), "tile", None, None),
            P("group", None, None),
            P("group", None),
            P("group", None),
            P("group"),
            P("group", None),
        ),
        check_vma=False,
    )
```

profile of v0, /device:TPU:0, one launch (start us, length us, event | category | flops | bytes accessed | tf_op | source)
XLA Modules:
  0.0 275.7 jit_solution(4740820683694021550)
XLA Ops:
  7.2 1.2 copy.24
  8.5 4.9 %collective-permute-start = (bf16[1,3,270,256]{3,2,1,0:T(8,128)(2,1)S(1)}, bf16[1,3,270,256]{3,2,1,0:T(8,128)(2,1)S(1)}, u32[]{:S(2)}, u32[]{:S(2)}) collective-permute-start(bf16[1,3,270,256]{3,2,1,0:T(8,128)(2,1)S(1)} %get-tuple-element.91), channel_id=1, source_target_pairs={{0,2},{2,4},{4,6},{6,8},{8,10},{10,12},{12,14},{1,3},{3,5},{5,7},{... | collective-permute-start | bytes 1244168 | tf_op jit(solution)/shard_map/ppermute | solution.py:19
  13.4 1.3 collective-permute-start.1
  15.0 16.2 %collective-permute-done = bf16[1,3,270,256]{3,2,1,0:T(8,128)(2,1)S(1)} collective-permute-done((bf16[1,3,270,256]{3,2,1,0:T(8,128)(2,1)S(1)}, bf16[1,3,270,256]{3,2,1,0:T(8,128)(2,1)S(1)}, u32[]{:S(2)}, u32[]{:S(2)}) %collective-permute-start) | collective-permute-done | bytes 414752 | tf_op jit(solution)/shard_map/ppermute | solution.py:19
  31.7 9.9 %fusion.233 = (f32[4,270]{1,0:T(4,128)S(1)}, f32[1,4,270,256]{3,2,1,0:T(8,128)S(1)}) fusion(f32[256]{0:T(256)S(1)} %copy-done.91, f32[256]{0:T(256)S(1)} %bitcast.185, f32[1,10,3,256]{3,2,1,0:T(4,128)S(1)} %get-tuple-element.84, f32[1,10,270,256]{3,2,1,0:T(8,128)S(1)} %maximum_convert_fusion, f32[256]{0:T(256)S(1)} %bitcast.187, f32[256]{0:T(256)S(1)} %bitcast.131, ...), kind=kLoop, calls=%fused_computation.447 | loop fusion | flops 38982600 | bytes 11827424 | tf_op jit(solution)/shard_map/reduce_sum | solution.py:87
  43.7 2.0 reshape.497
  45.7 4.8 %multiply_convert_fusion = (bf16[1080,1024]{1,0:T(8,128)(2,1)S(1)}, f32[1080,1024]{1,0:T(8,128)}) fusion(f32[1024]{0:T(1024)S(1)} %copy-done.96, bf16[1080,256]{1,0:T(8,128)(2,1)} %reshape.497, bf16[256,1024]{1,0:T(8,128)(2,1)S(1)} %copy-done), kind=kOutput, calls=%fused_computation.140 | convolution fusion | flops 577290240 | bytes 7716864 | tf_op jit(solution)/shard_map/dot_general | solution.py:92
  50.6 1.4 copy-done.99
  52.0 1.9 convolution_add_fusion.1
  53.8 2.5 reshape.498
  56.3 3.6 %fusion.11 = (f32[256]{0:T(256)}, bf16[1,4,270,256]{3,2,1,0:T(8,128)(2,1)}, f32[256]{0:T(256)}, bf16[1,4,270,256]{3,2,1,0:T(8,128)(2,1)}) fusion(f32[1,4,270,256]{3,2,1,0:T(8,128)} %reshape.498, f32[4,270]{1,0:T(4,128)S(1)} %convert_element_type.63, bf16[1,4,270,256]{3,1,2,0:T(4,128)(2,1)} %param.23, f32[256]{0:T(256)S(1)} %copy-done.93, ...), kind=kLoop, calls=%fused_computation.154 | loop fusion | flops 3593728 | bytes 3325152 | tf_op jit(solution)/shard_map/reduce_sum | solution.py:101
  60.0 2.0 reshape.499
  62.0 3.7 %fusion.242 = f32[1024,256]{1,0:T(8,128)} fusion(bf16[1080,1024]{1,0:T(8,128)(2,1)} %copy-done.99, bf16[1080,256]{1,0:T(8,128)(2,1)} %reshape.499), kind=kOutput, calls=%fused_computation.456 | convolution fusion | flops 566231040 | bytes 3813376 | tf_op jit(solution)/shard_map/dot_general | solution.py:104
  65.8 3.8 %convert_reduce_fusion.1 = (f32[1024]{0:T(1024)}, bf16[1080,1024]{1,0:T(8,128)(2,1)S(1)}) fusion(f32[1080,1024]{1,0:T(8,128)S(1)} %copy-done.100, bf16[1080,256]{1,0:T(8,128)(2,1)S(1)} %copy-done.8, bf16[1024,256]{1,0:T(8,128)(2,1)S(1)} %copy-done.95), kind=kOutput, calls=%fused_computation.139 | convolution fusion | flops 589454336 | bytes 7716864 | tf_op jit(solution)/shard_map/dot_general | solution.py:107
  69.6 1.4 copy-done.98
  71.0 1.9 fusion.241
  72.9 4.0 %fusion.231 = (f32[256]{0:T(256)}, f32[1080]{0:T(1024)S(1)}, f32[1080,256]{1,0:T(8,128)}) fusion(f32[256]{0:T(256)S(1)} %copy-done.10, bf16[1080,1024]{1,0:T(8,128)(2,1)} %copy-done.98, bf16[256,1024]{1,0:T(8,128)(2,1)S(1)} %copy-done), kind=kOutput, calls=%fused_computation.446 | convolution fusion | flops 567059136 | bytes 3848416 | tf_op jit(solution)/shard_map/dot_general | solution.py:115
  76.9 2.4 reshape.500
  79.2 2.7 multiply_reduce_fusion
  82.1 2.0 fusion.57
  84.1 2.1 fusion.55
  86.2 2.4 fusion.59
  88.6 2.3 fusion.60
  90.9 2.0 fusion.56
  92.9 2.5 fusion.58
  99.4 62.4 %all-reduce = (f32[7,7,256]{2,1,0:T(8,128)S(1)}, f32[1024]{0:T(1024)S(1)}, f32[5,256]{1,0:T(8,128)S(1)}) all-reduce(f32[7,7,256]{2,1,0:T(8,128)S(1)} %constant_dynamic-update-slice_fusion, f32[1024]{0:T(1024)S(1)} %copy-done.82, f32[5,256]{1,0:T(8,128)S(1)} %stack.279), channel_id=1, replica_groups=mesh['group'=2,'tile'=8,'draw'=2] {'tile','draw'}, use_global_device_ids=true, to_apply=%region_53.0 | all-reduce | flops 14848 | bytes 118784 | tf_op jit(solution)/shard_map/psum | solution.py:137
  162.4 1.3 collective-permute-start.2
  163.7 1.3 collective-permute-start.3
  167.6 13.8 %collective-permute-done.2 = bf16[1,3,270,256]{3,2,1,0:T(8,128)(2,1)S(1)} collective-permute-done((bf16[1,3,270,256]{3,2,1,0:T(8,128)(2,1)S(1)}, bf16[1,3,270,256]{3,2,1,0:T(8,128)(2,1)S(1)}, u32[]{:S(2)}, u32[]{:S(2)}) %collective-permute-start.2) | collective-permute-done | bytes 414752 | tf_op jit(solution)/shard_map/ppermute | solution.py:19
  181.9 9.5 %fusion.9 = bf16[1,4,270,256]{3,2,1,0:T(8,128)(2,1)S(1)} fusion(f32[1,10,3,256]{3,2,1,0:T(4,128)S(1)} %get-tuple-element.82, f32[1,10,270,256]{3,2,1,0:T(8,128)S(1)} %maximum_convert_fusion.1, f32[1,10,3,256]{3,2,1,0:T(4,128)S(1)} %get-tuple-element.81, f32[256]{0:T(256)S(1)} %bitcast.186, f32[256]{0:T(256)S(1)} %bitcast.188, f32[256]{0:T(256)S(1)} %bitcast.132, ...), kind=kLoop, calls=%fused_computation.152 | loop fusion | flops 39260160 | bytes 11822080 | tf_op jit(solution)/shard_map/convert_element_type | solution.py:133
  192.5 72.9 %all-reduce.4.cloned.1.call-done = (f32[256,1024]{1,0:T(8,128)}, f32[1024,256]{1,0:T(8,128)}) async-done(((f32[256,1024]{1,0:T(8,128)}, f32[1024,256]{1,0:T(8,128)}), (f32[256,1024]{1,0:T(8,128)}, f32[1024,256]{1,0:T(8,128)})) %all-reduce.4.cloned.1.call-update) | async-done | bytes 2097168 | tf_op jit(solution)/shard_map/psum | solution.py:137
  265.4 2.4 broadcast_multiply_fusion
  (242 shorter events, 11.6 us)
Async XLA Ops:
  7.2 38.5 %copy-start = (bf16[256,1024]{1,0:T(8,128)(2,1)S(1)}, bf16[256,1024]{1,0:T(8,128)(2,1)}, u32[]{:S(2)}) copy-start(bf16[256,1024]{1,0:T(8,128)(2,1)} %param.18) | copy-start | bytes 1572868
  7.2 258.2 %all-reduce.4.cloned.1.call-start = ((), (), s32[]{:S(2)}) async-start(), calls=%async_computation | async-start | bytes 4194304 | tf_op jit(solution)/shard_map/psum | solution.py:137
  8.5 22.7 %collective-permute-start = (bf16[1,3,270,256]{3,2,1,0:T(8,128)(2,1)S(1)}, bf16[1,3,270,256]{3,2,1,0:T(8,128)(2,1)S(1)}, u32[]{:S(2)}, u32[]{:S(2)}) collective-permute-start(bf16[1,3,270,256]{3,2,1,0:T(8,128)(2,1)S(1)} %get-tuple-element.91), channel_id=1, source_target_pairs={{0,2},{2,4},{4,6},{6,8},{8,10},{10,12},{12,14},{1,3},{3,5},{5,7},{... | collective-permute-start | bytes 1244168 | tf_op jit(solution)/shard_map/ppermute | solution.py:19
  13.4 17.8 %collective-permute-start.1 = (bf16[1,3,270,256]{3,2,1,0:T(8,128)(2,1)S(1)}, bf16[1,3,270,256]{3,2,1,0:T(8,128)(2,1)S(1)}, u32[]{:S(2)}, u32[]{:S(2)}) collective-permute-start(bf16[1,3,270,256]{3,2,1,0:T(8,128)(2,1)S(1)} %get-tuple-element.92), channel_id=1, source_target_pairs={{2,0},{4,2},{6,4},{8,6},{10,8},{12,10},{14,12},{3,1},{5,3},{7,5},{... | collective-permute-start | bytes 1244168 | tf_op jit(solution)/shard_map/ppermute | solution.py:21
  14.8 16.7 %copy-start.11 = (f32[1,1,256]{2,1,0:T(1,128)}, f32[1,1,256]{2,1,0:T(1,128)S(1)}, u32[]{:S(2)}) copy-start(f32[1,1,256]{2,1,0:T(1,128)S(1)} %get-tuple-element.141) | copy-start | bytes 3076
  14.8 16.7 %copy-start.13 = (f32[1,1,256]{2,1,0:T(1,128)}, f32[1,1,256]{2,1,0:T(1,128)S(1)}, u32[]{:S(2)}) copy-start(f32[1,1,256]{2,1,0:T(1,128)S(1)} %get-tuple-element.112) | copy-start | bytes 3076
  14.8 16.7 %copy-start.15 = (f32[1,1,256]{2,1,0:T(1,128)}, f32[1,1,256]{2,1,0:T(1,128)S(1)}, u32[]{:S(2)}) copy-start(f32[1,1,256]{2,1,0:T(1,128)S(1)} %get-tuple-element.113) | copy-start | bytes 3076
  14.8 16.7 %copy-start.17 = (f32[1,1,256]{2,1,0:T(1,128)}, f32[1,1,256]{2,1,0:T(1,128)S(1)}, u32[]{:S(2)}) copy-start(f32[1,1,256]{2,1,0:T(1,128)S(1)} %get-tuple-element.114) | copy-start | bytes 3076
  14.8 16.7 %copy-start.19 = (f32[1,1,256]{2,1,0:T(1,128)}, f32[1,1,256]{2,1,0:T(1,128)S(1)}, u32[]{:S(2)}) copy-start(f32[1,1,256]{2,1,0:T(1,128)S(1)} %get-tuple-element.115) | copy-start | bytes 3076
  14.9 16.7 %copy-start.21 = (f32[1,1,256]{2,1,0:T(1,128)}, f32[1,1,256]{2,1,0:T(1,128)S(1)}, u32[]{:S(2)}) copy-start(f32[1,1,256]{2,1,0:T(1,128)S(1)} %get-tuple-element.116) | copy-start | bytes 3076
  14.9 16.7 %copy-start.23 = (f32[1,1,256]{2,1,0:T(1,128)}, f32[1,1,256]{2,1,0:T(1,128)S(1)}, u32[]{:S(2)}) copy-start(f32[1,1,256]{2,1,0:T(1,128)S(1)} %get-tuple-element.117) | copy-start | bytes 3076
  14.9 16.7 %copy-start.25 = (f32[1,1,256]{2,1,0:T(1,128)}, f32[1,1,256]{2,1,0:T(1,128)S(1)}, u32[]{:S(2)}) copy-start(f32[1,1,256]{2,1,0:T(1,128)S(1)} %get-tuple-element.118) | copy-start | bytes 3076
  14.9 16.7 %copy-start.27 = (f32[1,1,256]{2,1,0:T(1,128)}, f32[1,1,256]{2,1,0:T(1,128)S(1)}, u32[]{:S(2)}) copy-start(f32[1,1,256]{2,1,0:T(1,128)S(1)} %get-tuple-element.119) | copy-start | bytes 3076
  14.9 16.7 %copy-start.29 = (f32[1,1,256]{2,1,0:T(1,128)}, f32[1,1,256]{2,1,0:T(1,128)S(1)}, u32[]{:S(2)}) copy-start(f32[1,1,256]{2,1,0:T(1,128)S(1)} %get-tuple-element.120) | copy-start | bytes 3076
  14.9 16.7 %copy-start.31 = (f32[1,1,256]{2,1,0:T(1,128)}, f32[1,1,256]{2,1,0:T(1,128)S(1)}, u32[]{:S(2)}) copy-start(f32[1,1,256]{2,1,0:T(1,128)S(1)} %get-tuple-element.121) | copy-start | bytes 3076
  14.9 16.7 %copy-start.33 = (f32[1,1,256]{2,1,0:T(1,128)}, f32[1,1,256]{2,1,0:T(1,128)S(1)}, u32[]{:S(2)}) copy-start(f32[1,1,256]{2,1,0:T(1,128)S(1)} %get-tuple-element.122) | copy-start | bytes 3076
  14.9 16.7 %copy-start.35 = (f32[1,1,256]{2,1,0:T(1,128)}, f32[1,1,256]{2,1,0:T(1,128)S(1)}, u32[]{:S(2)}) copy-start(f32[1,1,256]{2,1,0:T(1,128)S(1)} %get-tuple-element.123) | copy-start | bytes 3076
  14.9 16.7 %copy-start.37 = (f32[1,1,256]{2,1,0:T(1,128)}, f32[1,1,256]{2,1,0:T(1,128)S(1)}, u32[]{:S(2)}) copy-start(f32[1,1,256]{2,1,0:T(1,128)S(1)} %get-tuple-element.124) | copy-start | bytes 3076
  14.9 16.7 %copy-start.39 = (f32[1,1,256]{2,1,0:T(1,128)}, f32[1,1,256]{2,1,0:T(1,128)S(1)}, u32[]{:S(2)}) copy-start(f32[1,1,256]{2,1,0:T(1,128)S(1)} %get-tuple-element.125) | copy-start | bytes 3076
  15.0 16.7 %copy-start.41 = (f32[1,1,256]{2,1,0:T(1,128)}, f32[1,1,256]{2,1,0:T(1,128)S(1)}, u32[]{:S(2)}) copy-start(f32[1,1,256]{2,1,0:T(1,128)S(1)} %get-tuple-element.126) | copy-start | bytes 3076
  15.0 16.7 %copy-start.43 = (f32[1,1,256]{2,1,0:T(1,128)}, f32[1,1,256]{2,1,0:T(1,128)S(1)}, u32[]{:S(2)}) copy-start(f32[1,1,256]{2,1,0:T(1,128)S(1)} %get-tuple-element.127) | copy-start | bytes 3076
  15.0 16.7 %copy-start.45 = (f32[1,1,256]{2,1,0:T(1,128)}, f32[1,1,256]{2,1,0:T(1,128)S(1)}, u32[]{:S(2)}) copy-start(f32[1,1,256]{2,1,0:T(1,128)S(1)} %get-tuple-element.128) | copy-start | bytes 3076
  15.0 16.7 %copy-start.47 = (f32[1,1,256]{2,1,0:T(1,128)}, f32[1,1,256]{2,1,0:T(1,128)S(1)}, u32[]{:S(2)}) copy-start(f32[1,1,256]{2,1,0:T(1,128)S(1)} %get-tuple-element.129) | copy-start | bytes 3076
  15.0 16.7 %copy-start.49 = (f32[1,1,256]{2,1,0:T(1,128)}, f32[1,1,256]{2,1,0:T(1,128)S(1)}, u32[]{:S(2)}) copy-start(f32[1,1,256]{2,1,0:T(1,128)S(1)} %get-tuple-element.130) | copy-start | bytes 3076
  15.0 16.7 %copy-start.91 = (f32[256]{0:T(256)S(1)}, f32[256]{0:T(256)}, u32[]{:S(2)}) copy-start(f32[256]{0:T(256)} %param.15) | copy-start | bytes 3076
  95.8 69.2 %copy-start.4 = (bf16[1,4,270,256]{3,2,1,0:T(8,128)(2,1)S(1)}, bf16[1,4,270,256]{3,2,1,0:T(8,128)(2,1)}, u32[]{:S(2)}) copy-start(bf16[1,4,270,256]{3,2,1,0:T(8,128)(2,1)} %get-tuple-element.86) | copy-start | bytes 1658884
  162.4 19.0 %collective-permute-start.2 = (bf16[1,3,270,256]{3,2,1,0:T(8,128)(2,1)S(1)}, bf16[1,3,270,256]{3,2,1,0:T(8,128)(2,1)S(1)}, u32[]{:S(2)}, u32[]{:S(2)}) collective-permute-start(bf16[1,3,270,256]{3,2,1,0:T(8,128)(2,1)S(1)} %get-tuple-element.89), channel_id=1, source_target_pairs={{0,2},{2,4},{4,6},{6,8},{8,10},{10,12},{12,14},{1,3},{3,5},{5,7},{... | collective-permute-start | bytes 1244168 | tf_op jit(solution)/shard_map/ppermute | solution.py:19
  163.7 17.7 %collective-permute-start.3 = (bf16[1,3,270,256]{3,2,1,0:T(8,128)(2,1)S(1)}, bf16[1,3,270,256]{3,2,1,0:T(8,128)(2,1)S(1)}, u32[]{:S(2)}, u32[]{:S(2)}) collective-permute-start(bf16[1,3,270,256]{3,2,1,0:T(8,128)(2,1)S(1)} %get-tuple-element.90), channel_id=1, source_target_pairs={{2,0},{4,2},{6,4},{8,6},{10,8},{12,10},{14,12},{3,1},{5,3},{7,5},{... | collective-permute-start | bytes 1244168 | tf_op jit(solution)/shard_map/ppermute | solution.py:21
  166.1 15.3 %copy-start.2 = (bf16[1,4,270,256]{3,2,1,0:T(8,128)(2,1)S(1)}, bf16[1,4,270,256]{3,2,1,0:T(8,128)(2,1)}, u32[]{:S(2)}) copy-start(bf16[1,4,270,256]{3,2,1,0:T(8,128)(2,1)} %copy-done.1) | copy-start | bytes 1658884
  167.4 14.3 %copy-start.18 = (f32[1,1,256]{2,1,0:T(1,128)S(1)}, f32[1,1,256]{2,1,0:T(1,128)}, u32[]{:S(2)}) copy-start(f32[1,1,256]{2,1,0:T(1,128)} %copy-done.17) | copy-start | bytes 3076
  167.4 14.3 %copy-start.20 = (f32[1,1,256]{2,1,0:T(1,128)S(1)}, f32[1,1,256]{2,1,0:T(1,128)}, u32[]{:S(2)}) copy-start(f32[1,1,256]{2,1,0:T(1,128)} %copy-done.19) | copy-start | bytes 3076
  167.4 14.3 %copy-start.22 = (f32[1,1,256]{2,1,0:T(1,128)S(1)}, f32[1,1,256]{2,1,0:T(1,128)}, u32[]{:S(2)}) copy-start(f32[1,1,256]{2,1,0:T(1,128)} %copy-done.21) | copy-start | bytes 3076
  (74 other events, 410.8 us)
Sparse Core Ops, SparseCore 0:
  166.3 99.0 all-reduce.3
where the time goes:
time: 276 us
  waiting for transfers between devices  103 us (37%)
  blocking collectives  62.4 us (23%)
  other arithmetic  46.5 us (17%)
  matrix products  20.2 us (7%)
  local copies, waits for them, and re-layouts  19.3 us (7%)
  between operations  15.5 us (6%)
  starting transfers between devices  8.82 us (3%)
    psum x1, waiting for transfers between devices, per_device(): lax.psum((kernel_part, w_in_part, w_out_part, hidden_bias_part, channel_p...  72.9 us
    psum x1, blocking collectives, per_device(): lax.psum((kernel_part, w_in_part, w_out_part, hidden_bias_part, channel_p...  62.4 us
    ppermute x2, waiting for transfers between devices, with_halo(): lax.ppermute(tail, axis, [(i, (i + 1) % count) for i in range(ends)])  30 us
    reduce_sum x6, other arithmetic, kernel_terms(): cells_list.append(jnp.sum(window * grad_map, axis=(0, 1, 2)))  13.4 us
    reduce_sum x1, other arithmetic, per_device(): center = jnp.mean(conv_out, axis=-1, keepdims=True)  9.86 us
    convert_element_type x1, other arithmetic, per_device(): (upstream + apply_taps(grad_padded, kernel[::-1, ::-1], height, breadth))...  9.55 us
    unnamed x211, local copies, waits for them, and re-layouts  7.31 us
    ppermute x2, starting transfers between devices, with_halo(): lax.ppermute(tail, axis, [(i, (i + 1) % count) for i in range(ends)])  6.2 us
  transfers between devices with their start and end apart: 5, of which 3 were waited for; matrix products, arithmetic and copies ran while one was open for 5% of the time, Pallas kernels for 0%

commit v1 on v0

v1 whole, which is shorter than its diff:
```python
import functools

import jax
import jax.numpy as jnp
from jax import lax
from jax.experimental import pallas as pl
from jax.experimental.pallas import tpu as pltpu
from jax.sharding import PartitionSpec as P

ROOT_TERM = 0.7978845608028654
CUBIC = 0.044715
EPSILON = 1e-06
F32 = jnp.float32
BF16 = jnp.bfloat16


def block_kernel(
    n,
    scale,
    x_ref,
    cot_ref,
    mask_ref,
    taps_ref,
    conv_bias_ref,
    gain_ref,
    nbias_ref,
    w_in_ref,
    b_in_ref,
    w_out_ref,
    b_out_ref,
    ls_ref,
    out_ref,
    igrad_ref,
    wi_ref,
    wo_ref,
    small_ref,
    xo,
    x_top,
    x_bot,
    cot,
    wrap,
    xs,
    gs,
    acc,
    hid,
    gact,
    act,
    gh,
    normed,
    gmix,
    gb,
    g_top,
    g_bot,
    gf,
    bsum,
    chan,
    part,
    r1,
    r2,
    r3,
    whole,
    sm,
    s1,
    s2,
    s3,
    s5,
    s6,
    halo_send,
    halo_recv,
    send_sem,
    recv_sem,
    z_send,
    z_recv,
):
    H, W, C = x_ref.shape
    Wp = xo.shape[1]
    B = Wp // 8
    HID = w_in_ref.shape[1]
    m = n // 2
    g = lax.axis_index("group")
    t = lax.axis_index("tile")
    d = lax.axis_index("draw")
    zz = t // 2
    yy = lax.rem(t, 2)
    ty = t + 1 - 2 * yy
    core = (g, t, 1 - d)
    beside = (g, ty, d)
    up = (g, lax.rem(t + n - 1, n), d)
    down = (g, lax.rem(t + 1, n), d)
    zpeer = [(g, 2 * lax.rem(zz + k, m) + yy, d) for k in range(m)]

    def remote(src, dst, ss, rs, dev):
        return pltpu.make_async_remote_copy(
            src_ref=src,
            dst_ref=dst,
            send_sem=ss,
            recv_sem=rs,
            device_id=dev,
            device_id_type=pl.DeviceIdType.MESH,
        )

    barrier = pltpu.get_barrier_semaphore()
    for dev in [core, up, down] + zpeer[1:]:
        pl.semaphore_signal(barrier, inc=1, device_id=dev, device_id_type=pl.DeviceIdType.MESH)
    for p in range(H):
        xo[p, 0:W] = x_ref[p]
        xo[p, W:Wp] = jnp.zeros((Wp - W, C), BF16)
    pl.semaphore_wait(barrier, m + 2)

    def halo(own, top, bot, at):
        to_up = remote(own.at[0:3], bot, halo_send.at[at], halo_recv.at[at], up)
        to_down = remote(own.at[H - 3 : H], top, halo_send.at[at + 1], halo_recv.at[at + 1], down)
        return to_up, to_down

    def halo_wait(pair, top, bot):
        to_up, to_down = pair

        @pl.when(t > 0)
        def _():
            to_up.wait_send()
            to_down.wait_recv()

        @pl.when(t < n - 1)
        def _():
            to_down.wait_send()
            to_up.wait_recv()

        @pl.when(t == 0)
        def _():
            top[...] = jnp.zeros_like(top)

        @pl.when(t == n - 1)
        def _():
            bot[...] = jnp.zeros_like(bot)

    x_halo = halo(xo, x_top, x_bot, 0)

    @pl.when(t > 0)
    def _():
        x_halo[0].start()

    @pl.when(t < n - 1)
    def _():
        x_halo[1].start()

    def spread(value, dst, row):
        v = value.astype(F32)
        wrap[8 : 8 + Wp] = v
        wrap[5:8] = v[W - 3 : W]
        wrap[8 + W : 16 + W] = v[0:8]
        for j in range(7):
            dst[j, row] = wrap[5 + j : 5 + j + Wp].reshape(B, 8, C)

    def own_spread(own, dst):
        @pl.loop(0, H)
        def _(r):
            spread(own[r], dst, r + 3)

    def halo_spread(top, bot, dst):
        @pl.loop(0, 3)
        def _(r):
            spread(top[r], dst, r)
            spread(bot[r], dst, r + H + 3)

    def conv(src, rows, flip, first):
        @pl.loop(0, B // 2)
        def _(c):
            q = pl.ds(c * 2, 2)
            sums = [None if first else acc[p, q] for p in range(H)]
            for j in range(7):
                for r in rows:
                    cells = src[j, r, q]
                    for p in range(H):
                        i = r - p
                        if 0 <= i < 7:
                            tap = (6 - i) * 7 + 6 - j if flip else i * 7 + j
                            term = cells * taps_ref[tap][None]
                            sums[p] = term if sums[p] is None else sums[p] + term
            for p in range(H):
                acc[p, q] = sums[p]

    own_rows = list(range(3, H + 3))
    halo_rows = [0, 1, 2] + list(range(H + 3, H + 6))
    own_spread(xo, xs)
    conv(xs, own_rows, False, True)
    for p in range(H):
        cot[p, 0:W] = cot_ref[p].astype(F32)
        cot[p, W:Wp] = jnp.zeros((Wp - W, C), F32)
    bsum[...] = jnp.zeros_like(bsum)
    chan[...] = jnp.zeros_like(chan)
    halo_wait(x_halo, x_top, x_bot)
    halo_spread(x_top, x_bot, xs)
    conv(xs, halo_rows, False, False)

    def rowsum(v):
        return jnp.sum(v, axis=0, keepdims=True)

    @pl.loop(0, H)
    def _(p):
        conv_out = acc[p].reshape(Wp, C) + conv_bias_ref[...]
        dev = conv_out - jnp.mean(conv_out, axis=-1, keepdims=True)
        rstd = lax.rsqrt(jnp.mean(dev * dev, axis=-1, keepdims=True) + EPSILON)
        unit = dev * rstd
        gf[p] = unit
        normed[p] = (unit * gain_ref[...] + nbias_ref[...]).astype(BF16)
        hid[...] = jnp.dot(normed[p], w_in_ref[...], preferred_element_type=F32)
        ocean = mask_ref[p].astype(F32)
        grad_mixed = (ocean * ls_ref[...] * cot[p]).astype(BF16)
        gmix[p] = grad_mixed
        gact[...] = lax.dot_general(
            grad_mixed, w_out_ref[...], (((1,), (1,)), ((), ())), preferred_element_type=F32
        )

        @pl.loop(0, Wp // 16)
        def _(c):
            q = pl.ds(pl.multiple_of(c * 16, 16), 16)
            h = hid[q] + b_in_ref[...]
            h2 = h * h
            th = jnp.tanh(ROOT_TERM * (h + CUBIC * h2 * h))
            half = 0.5 * (1.0 + th)
            act[p, q] = (h * half).astype(BF16)
            slope = half + 0.5 * h * (1.0 - th * th) * ROOT_TERM * (1.0 + 3.0 * CUBIC * h2)
            grad_hidden = (gact[q] * slope).astype(BF16)
            gh[p, q] = grad_hidden
            wide = grad_hidden.astype(F32)
            bsum[...] += wide[0:8] + wide[8:16]

        mixed = jnp.dot(act[p], w_out_ref[...], preferred_element_type=F32) + b_out_ref[...]
        out_ref[p] = (xo[p].astype(F32) + ocean * ls_ref[...] * mixed).astype(BF16)[0:W]
        grad_normed = lax.dot_general(
            gh[p], w_in_ref[...], (((1,), (1,)), ((), ())), preferred_element_type=F32
        )
        unit = gf[p]
        scaled = grad_normed * gain_ref[...]
        grad_conv = rstd * (
            scaled
            - jnp.mean(scaled, axis=-1, keepdims=True)
            - unit * jnp.mean(scaled * unit, axis=-1, keepdims=True)
        )
        rounded = grad_conv.astype(BF16)
        gb[p] = rounded
        chan[0:1] += rowsum(rounded.astype(F32))
        chan[1:2] += rowsum(grad_normed * unit)
        chan[2:3] += rowsum(grad_normed)
        chan[3:4] += rowsum(gmix[p].astype(F32))
        chan[4:5] += rowsum(ocean * cot[p] * mixed)

    g_halo = halo(gb, g_top, g_bot, 2)

    @pl.when(t > 0)
    def _():
        g_halo[0].start()

    @pl.when(t < n - 1)
    def _():
        g_halo[1].start()

    flat = H * Wp
    tiles = part.shape[0] * part.shape[1] * part.shape[2] * part.shape[3]
    T = part.shape[3]
    d_in = lax.dot_general(
        normed[...].reshape(flat, C),
        gh[...].reshape(flat, HID),
        (((0,), (0,)), ((), ())),
        preferred_element_type=F32,
    )
    per = C // 16
    for cb in range(HID // C):
        for rb in range(per):
            k = cb * per + rb
            part[k // (tiles // 2), k // (tiles // 4) % 2, k // T % m, k % T, 0:16] = d_in[
                rb * 16 : rb * 16 + 16, cb * C : cb * C + C
            ].astype(BF16)
    d_out = lax.dot_general(
        gmix[...].reshape(flat, C),
        act[...].reshape(flat, HID),
        (((0,), (0,)), ((), ())),
        preferred_element_type=F32,
    ).T
    for k in range(tiles):
        part[k // (tiles // 2), k // (tiles // 4) % 2, k // T % m, k % T, 16:32] = d_out[
            k * 16 : k * 16 + 16
        ].astype(BF16)

    step1 = remote(part.at[1 - d], r1, send_sem.at[0], recv_sem.at[0], core)
    step1.start()

    own_spread(gb, gs)
    conv(gs, own_rows, True, True)

    step1.wait()
    r1[...] = (part[d].astype(F32) + r1[...].astype(F32)).astype(BF16)
    step2 = remote(r1.at[1 - yy], r2, send_sem.at[1], recv_sem.at[1], beside)
    step2.start()

    for j in range(7):

        def tap_terms(c, sums):
            q = pl.ds(c * 2, 2)
            cells16 = pl.ds(pl.multiple_of(c * 16, 16), 16)
            grads = [gb[p, cells16].astype(F32).reshape(2, 8, C) for p in range(H)]
            sums = list(sums)
            for r in range(H + 6):
                cells = xs[j, r, q]
                for p in range(H):
                    i = r - p
                    if 0 <= i < 7:
                        term = cells * grads[p]
                        sums[i] = sums[i] + (term[0] + term[1])
            return tuple(sums)

        sums = lax.fori_loop(0, B // 2, tap_terms, tuple(jnp.zeros((8, C), F32) for _ in range(7)))
        for i in range(7):
            k = i * 7 + j
            sm[k // 32, k % 32 : k % 32 + 1] = rowsum(sums[i])
    hidden_sum = rowsum(bsum[...])
    for k in range(HID // C):
        sm[1, 17 + k : 18 + k] = hidden_sum[:, k * C : k * C + C]
    sm[1, 21:26] = chan[0:5]
    sm[1, 26:32] = jnp.zeros((6, C), F32)

    small1 = remote(sm.at[1 - d], s1, send_sem.at[4], recv_sem.at[4], core)
    small1.start()
    step2.wait()
    r2[...] = (r1[yy].astype(F32) + r2[...].astype(F32)).astype(BF16)
    step3 = [
        remote(r2.at[lax.rem(zz + k, m)], r3.at[k - 1], z_send.at[k - 1], z_recv.at[k - 1], zpeer[k])
        for k in range(1, m)
    ]
    for copy in step3:
        copy.start()
    small1.wait()
    s2[...] = sm[d] + s1[...]
    small2 = remote(s2, s3, send_sem.at[5], recv_sem.at[5], beside)
    small2.start()

    halo_wait(g_halo, g_top, g_bot)
    halo_spread(g_top, g_bot, gs)

    for copy in step3:
        copy.wait()
    total = r2[zz].astype(F32)
    for k in range(m - 1):
        total = total + r3[k].astype(F32)
    whole[d, yy, zz] = (total * scale).astype(BF16)
    mine = whole.at[d, yy, zz]
    step4 = [
        remote(mine, mine, z_send.at[m - 2 + k], z_recv.at[m - 2 + k], zpeer[k])
        for k in range(1, m)
    ]
    for copy in step4:
        copy.start()
    small2.wait()
    s5[zz] = s2[...] + s3[...]
    small3 = [
        remote(s5.at[zz], s5.at[zz], z_send.at[2 * m - 3 + k], z_recv.at[2 * m - 3 + k], zpeer[k])
        for k in range(1, m)
    ]
    for copy in small3:
        copy.start()

    conv(gs, halo_rows, True, False)

    for copy in step4:
        copy.wait()
    step5 = remote(
        whole.at[d, yy], whole.at[d, yy], send_sem.at[2], recv_sem.at[2], beside
    )
    step5.start()
    for copy in small3:
        copy.wait()
    small_total = s5[0]
    for k in range(1, m):
        small_total = small_total + s5[k]
    s6[d] = small_total * scale
    small4 = remote(s6.at[d], s6.at[d], send_sem.at[6], recv_sem.at[6], core)
    small4.start()
    for p in range(H):
        igrad_ref[p] = (cot[p] + acc[p].reshape(Wp, C)).astype(BF16)[0:W]
    step5.wait()
    step6 = remote(whole.at[d], whole.at[d], send_sem.at[3], recv_sem.at[3], core)
    step6.start()
    small4.wait()
    small_ref[...] = s6[...]
    step6.wait()
    for cb in range(HID // C):
        for rb in range(per):
            k = cb * per + rb
            wi_ref[rb * 16 : rb * 16 + 16, cb * C : cb * C + C] = whole[
                k // (tiles // 2), k // (tiles // 4) % 2, k // T % m, k % T, 0:16
            ].astype(F32)
    for k in range(tiles):
        wo_ref[k * 16 : k * 16 + 16] = whole[
            k // (tiles // 2), k // (tiles // 4) % 2, k // T % m, k % T, 16:32
        ].astype(F32)


def per_device(
    n,
    draws,
    inputs,
    land_mask,
    kernel,
    conv_bias,
    norm_gain,
    norm_bias,
    w_in,
    b_in,
    w_out,
    b_out,
    layer_scale,
    cotangent,
):
    _, H, W, C = inputs.shape
    HID = w_in.shape[1]
    Wp = (W + 15) // 16 * 16
    B = Wp // 8
    m = n // 2
    T = HID // 16 // (2 * n)
    scale = float(1.0 / (draws * H * n * W) ** 0.5)
    ocean = jnp.broadcast_to(
        jnp.pad(land_mask, ((0, 0), (0, Wp - W))).astype(BF16)[:, :, None], (H, Wp, C)
    )
    taps = jnp.broadcast_to(kernel.reshape(49, 1, C), (49, 8, C))
    vm = pl.BlockSpec(memory_space=pltpu.VMEM)
    scratch = [
        ((H, Wp, C), BF16),
        ((3, Wp, C), BF16),
        ((3, Wp, C), BF16),
        ((H, Wp, C), F32),
        ((Wp + 16, C), F32),
        ((7, H + 6, B, 8, C), F32),
        ((7, H + 6, B, 8, C), F32),
        ((H, B, 8, C), F32),
        ((Wp, HID), F32),
        ((Wp, HID), F32),
        ((H, Wp, HID), BF16),
        ((H, Wp, HID), BF16),
        ((H, Wp, C), BF16),
        ((H, Wp, C), BF16),
        ((H, Wp, C), BF16),
        ((3, Wp, C), BF16),
        ((3, Wp, C), BF16),
        ((H, Wp, C), F32),
        ((8, HID), F32),
        ((8, C), F32),
        ((2, 2, m, T, 32, C), BF16),
        ((2, m, T, 32, C), BF16),
        ((m, T, 32, C), BF16),
        ((m - 1, T, 32, C), BF16),
        ((2, 2, m, T, 32, C), BF16),
        ((2, 32, C), F32),
        ((32, C), F32),
        ((32, C), F32),
        ((32, C), F32),
        ((m, 32, C), F32),
        ((2, 32, C), F32),
    ]
    output, input_grad, w_in_grad, w_out_grad, small = pl.pallas_call(
        functools.partial(block_kernel, n, scale),
        out_shape=(
            jax.ShapeDtypeStruct((H, W, C), BF16),
            jax.ShapeDtypeStruct((H, W, C), BF16),
            jax.ShapeDtypeStruct((C, HID), F32),
            jax.ShapeDtypeStruct((HID, C), F32),
            jax.ShapeDtypeStruct((2, 32, C), F32),
        ),
        in_specs=[vm] * 12,
        out_specs=[vm] * 5,
        scratch_shapes=[pltpu.VMEM(shape, dtype) for shape, dtype in scratch]
        + [
            pltpu.SemaphoreType.DMA((4,)),
            pltpu.SemaphoreType.DMA((4,)),
            pltpu.SemaphoreType.DMA((7,)),
            pltpu.SemaphoreType.DMA((7,)),
            pltpu.SemaphoreType.DMA((3 * (m - 1),)),
            pltpu.SemaphoreType.DMA((3 * (m - 1),)),
        ],
        compiler_params=pltpu.CompilerParams(
            collective_id=0, has_side_effects=True, vmem_limit_bytes=62 * 1024 * 1024
        ),
    )(
        inputs[0],
        cotangent[0],
        ocean,
        taps,
        conv_bias[None],
        norm_gain[None],
        norm_bias[None],
        w_in,
        b_in[None],
        w_out,
        b_out[None],
        layer_scale[None],
    )
    rows = small.reshape(64, C)
    return (
        output[None],
        input_grad[None],
        rows[0:49].reshape(7, 7, C),
        w_in_grad,
        w_out_grad,
        rows[49 : 49 + HID // C].reshape(HID),
        rows[49 + HID // C : 54 + HID // C],
    )


def solution(mesh):
    field = P(("group", "draw"), "tile", None, None)
    placed = (field, P("tile", None)) + (P(),) * 9 + (field,)
    return jax.shard_map(
        functools.partial(per_device, mesh.shape["tile"], mesh.shape["draw"]),
        mesh=mesh,
        in_specs=placed,
        out_specs=(
            field,
            field,
            P("group", None, None),
            P("group", None),
            P("group", None),
            P("group"),
            P("group", None),
        ),
        check_vma=False,
    )
```

time: 276 us -> 99.4 us (0.36)
  waiting for transfers between devices: 103 us -> 0 us
  Pallas kernels: 0 us -> 86.1 us
  blocking collectives: 62.4 us -> 0 us
  other arithmetic: 46.5 us -> 0.01 us
  matrix products: 20.2 us -> 0 us
  between operations: 15.5 us -> 0.69 us
  starting transfers between devices: 8.82 us -> 0 us
  local copies, waits for them, and re-layouts: 19.3 us -> 12.3 us
    pallas_call x0 -> x1, Pallas kernels: none -> 86.1 us  [per_device(): pl.pallas_call(functools.partial(block_kernel, n, scale), out_shape=(jax....]
    psum x1 -> x0, waiting for transfers between devices: 72.9 us -> none  [per_device(): lax.psum((kernel_part, w_in_part, w_out_part, hidden_bias_part, channel_p...]
    psum x1 -> x0, blocking collectives: 62.4 us -> none  [per_device(): lax.psum((kernel_part, w_in_part, w_out_part, hidden_bias_part, channel_p...]
    reduce_sum x10 -> x0, other arithmetic: 30.1 us -> none  [the longest x6 13.4 us: kernel_terms(): cells_list.append(jnp.sum(window * grad_map, axis=(0, 1, 2)))]
    ppermute x4 -> x0, waiting for transfers between devices: 30 us -> none  [the longest x2 30 us: with_halo(): lax.ppermute(tail, axis, [(i, (i + 1) % count) for i in range(ends)])]
    dot_general x6 -> x0, matrix products: 20.2 us -> none  [the longest x1 4.84 us: per_device(): hidden = jnp.dot(normed, w_in, preferred_element_type=jnp.float32) + b_in]
    convert_element_type x5 -> x0, other arithmetic: 11.1 us -> none  [the longest x1 9.55 us: per_device(): (upstream + apply_taps(grad_padded, kernel[::-1, ::-1], height, breadth))...]
    ppermute x4 -> x0, starting transfers between devices: 8.78 us -> none  [the longest x2 6.2 us: with_halo(): lax.ppermute(tail, axis, [(i, (i + 1) % count) for i in range(ends)])]
  transfers between devices with their start and end apart: 5 -> 0, of which waited for: 3 -> 0; matrix products, arithmetic and copies ran while one was open for 5% -> 0% of each run, Pallas kernels for 0% -> 0%
where the time goes in v1:
time: 99.4 us; the launch traced here: 99.1 us
  Pallas kernels  86.1 us (87%)
  local copies, waits for them, and re-layouts  12.3 us (12%)
    pallas_call x1, Pallas kernels, per_device(): pl.pallas_call(functools.partial(block_kernel, n, scale), out_shape=(jax....  86.1 us
    unnamed x20, local copies, waits for them, and re-layouts  7.23 us

profile of v1, /device:TPU:0, one launch (start us, length us, event | category | flops | bytes accessed | tf_op | source)
XLA Modules:
  0.0 99.1 jit_solution(17564713065267508213)
XLA Ops:
  0.6 0.0 copy-start.6
  0.6 0.7 copy-done.6
  1.3 0.0 copy-start.3
  1.4 0.0 copy-start.4
  1.4 0.9 broadcast_in_dim.38
  2.3 0.8 broadcast_in_dim.39.taps_ref
  3.1 1.0 %broadcast_in_dim.37.mask_ref = bf16[4,272,256]{2,1,0:T(8,128)(2,1)} broadcast(bf16[4,272]{1,0:T(4,128)(2,1)S(1)} %pad.5), dimensions={0,1} | broadcast | bytes 559232 | tf_op jit(solution)/shard_map/broadcast_in_dim | solution.py:421
  4.1 0.0 copy-done.3
  4.1 0.0 copy-done.4
  4.1 1.1 %copy_bitcast_fusion = (bf16[4,270,256]{2,1,0:T(8,128)(2,1)}, bf16[4,270,256]{2,1,0:T(8,128)(2,1)}) fusion(bf16[1,4,270,256]{3,1,2,0:T(4,128)(2,1)S(1)} %copy-done.3, bf16[1,4,270,256]{3,1,2,0:T(4,128)(2,1)S(1)} %copy-done.4), kind=kLoop, calls=%fused_computation | loop fusion | bytes 2211840 | tf_op jit(solution)/shard_map/squeeze | solution.py:484
  5.2 86.1 %shard_map.171 = (bf16[4,270,256]{2,1,0:T(8,128)(2,1)}, bf16[4,270,256]{2,1,0:T(8,128)(2,1)}, f32[256,1024]{1,0:T(8,128)}, f32[1024,256]{1,0:T(8,128)}, f32[2,32,256]{2,1,0:T(8,128)}) custom-call(bf16[4,270,256]{2,1,0:T(8,128)(2,1)} %get-tuple-element.25.x_ref, bf16[4,270,256]{2,1,0:T(8,128)(2,1)} %get-tuple-element.24.cot_ref, ...), custom_call_target="tpu_custom_call" | custom-call | tf_op jit(solution)/shard_map/pallas_call | solution.py:459
  91.3 0.0 copy-start.2
  91.3 0.0 copy-start.1
  91.3 2.3 %copy.21 = bf16[1,4,270,256]{3,1,2,0:T(4,128)(2,1)} copy(bf16[1,4,270,256]{3,2,1,0:T(8,128)(2,1)} %bitcast.17) | data formatting | bytes 1105920
  93.6 0.0 copy-done.2
  93.6 0.0 copy-start.5
  93.6 1.1 %copy.22 = bf16[1,4,270,256]{3,1,2,0:T(4,128)(2,1)} copy(bf16[1,4,270,256]{3,2,1,0:T(8,128)(2,1)S(1)} %bitcast.16) | data formatting | bytes 1105920
  94.7 0.0 copy-done.5
  94.7 0.6 copy.23
  95.3 0.6 slice.14
  95.9 0.6 reshape.27
  96.5 0.0 copy-done.1
  96.5 0.0 copy-start
  96.5 1.0 copy.28
  97.5 0.6 copy-done
  98.2 1.0 copy.29
  (4 shorter events, 0.0 us)
Async XLA Ops:
  0.6 0.7 copy-start.6
  1.3 2.7 %copy-start.3 = (bf16[1,4,270,256]{3,1,2,0:T(4,128)(2,1)S(1)}, bf16[1,4,270,256]{3,1,2,0:T(4,128)(2,1)}, u32[]{:S(2)}) copy-start(bf16[1,4,270,256]{3,1,2,0:T(4,128)(2,1)} %param.23) | copy-start | bytes 1658884
  1.4 2.7 %copy-start.4 = (bf16[1,4,270,256]{3,1,2,0:T(4,128)(2,1)S(1)}, bf16[1,4,270,256]{3,1,2,0:T(4,128)(2,1)}, u32[]{:S(2)}) copy-start(bf16[1,4,270,256]{3,1,2,0:T(4,128)(2,1)} %param.12) | copy-start | bytes 1658884
  91.3 2.3 %copy-start.2 = (bf16[4,270,256]{2,1,0:T(8,128)(2,1)S(1)}, bf16[4,270,256]{2,1,0:T(8,128)(2,1)}, u32[]{:S(2)}) copy-start(bf16[4,270,256]{2,1,0:T(8,128)(2,1)} %get-tuple-element.13) | copy-start | bytes 1658884
  91.3 5.2 %copy-start.1 = (f32[256,1024]{1,0:T(8,128)S(1)}, f32[256,1024]{1,0:T(8,128)}, u32[]{:S(2)}) copy-start(f32[256,1024]{1,0:T(8,128)} %get-tuple-element.36) | copy-start | bytes 3145732
  93.6 1.1 %copy-start.5 = (f32[2,32,256]{2,1,0:T(8,128)S(1)}, f32[2,32,256]{2,1,0:T(8,128)}, u32[]{:S(2)}) copy-start(f32[2,32,256]{2,1,0:T(8,128)} %get-tuple-element.14) | copy-start | bytes 196612
  96.5 1.6 %copy-start = (f32[1024,256]{1,0:T(8,128)S(1)}, f32[1024,256]{1,0:T(8,128)}, u32[]{:S(2)}) copy-start(f32[1024,256]{1,0:T(8,128)} %get-tuple-element.37) | copy-start | bytes 3145732

commit v2 on v1

--- a/solution.py
+++ b/solution.py
@@ -33,14 +33,15 @@
     igrad_ref,
     wi_ref,
     wo_ref,
-    small_ref,
+    kgrad_ref,
+    bgrad_ref,
+    chan_ref,
     xo,
     x_top,
     x_bot,
     cot,
     wrap,
     xs,
-    gs,
     acc,
     hid,
     gact,
@@ -107,41 +108,61 @@
         xo[p, W:Wp] = jnp.zeros((Wp - W, C), BF16)
     pl.semaphore_wait(barrier, m + 2)
 
-    def halo(own, top, bot, at):
-        to_up = remote(own.at[0:3], bot, halo_send.at[at], halo_recv.at[at], up)
-        to_down = remote(own.at[H - 3 : H], top, halo_send.at[at + 1], halo_recv.at[at + 1], down)
-        return to_up, to_down
-
-    def halo_wait(pair, top, bot):
-        to_up, to_down = pair
-
+    @pl.when(t == 0)
+    def _():
+        x_top[...] = jnp.zeros_like(x_top)
+        g_top[...] = jnp.zeros_like(g_top)
+
+    @pl.when(t == n - 1)
+    def _():
+        x_bot[...] = jnp.zeros_like(x_bot)
+        g_bot[...] = jnp.zeros_like(g_bot)
+
+    def to_up(own, bot, a, at):
+        k = at + a
+        return remote(own.at[a], bot.at[a], halo_send.at[k], halo_recv.at[k], up)
+
+    def to_down(own, top, a, at):
+        k = at + 3 + a
+        return remote(own.at[H - 3 + a], top.at[a], halo_send.at[k], halo_recv.at[k], down)
+
+    def halo_start(own, top, bot, at, ups, downs):
         @pl.when(t > 0)
         def _():
-            to_up.wait_send()
-            to_down.wait_recv()
+            for a in ups:
+                to_up(own, bot, a, at).start()
 
         @pl.when(t < n - 1)
         def _():
-            to_down.wait_send()
-            to_up.wait_recv()
-
-        @pl.when(t == 0)
+            for a in downs:
+                to_down(own, top, a, at).start()
+
+    def halo_arrive(own, top, bot, at, ups, downs):
+        @pl.when(t > 0)
         def _():
-            top[...] = jnp.zeros_like(top)
-
-        @pl.when(t == n - 1)
+            for a in downs:
+                to_down(own, top, a, at).wait_recv()
+
+        @pl.when(t < n - 1)
         def _():
-            bot[...] = jnp.zeros_like(bot)
-
-    x_halo = halo(xo, x_top, x_bot, 0)
-
-    @pl.when(t > 0)
-    def _():
-        x_halo[0].start()
-
-    @pl.when(t < n - 1)
-    def _():
-        x_halo[1].start()
+            for a in ups:
+                to_up(own, bot, a, at).wait_recv()
+
+    def halo_sent(own, top, bot, at):
+        @pl.when(t > 0)
+        def _():
+            for a in range(3):
+                to_up(own, bot, a, at).wait_send()
+
+        @pl.when(t < n - 1)
+        def _():
+            for a in range(3):
+                to_down(own, top, a, at).wait_send()
+
+    x_side = (xo, x_top, x_bot, 0)
+    g_side = (gb, g_top, g_bot, 6)
+    for a in range(3):
+        halo_start(*x_side, [a], [2 - a])
 
     def spread(value, dst, row):
         v = value.astype(F32)
@@ -156,17 +177,18 @@
         def _(r):
             spread(own[r], dst, r + 3)
 
-    def halo_spread(top, bot, dst):
-        @pl.loop(0, 3)
-        def _(r):
-            spread(top[r], dst, r)
-            spread(bot[r], dst, r + H + 3)
+    def halo_spread(top, bot, dst, ups, downs):
+        for a in downs:
+            spread(top[a], dst, a)
+        for a in ups:
+            spread(bot[a], dst, a + H + 3)
 
     def conv(src, rows, flip, first):
         @pl.loop(0, B // 2)
         def _(c):
             q = pl.ds(c * 2, 2)
-            sums = [None if first else acc[p, q] for p in range(H)]
+            live = [p for p in range(H) if any(0 <= r - p < 7 for r in rows)]
+            sums = [acc[p, q] if p in live and not first else None for p in range(H)]
             for j in range(7):
                 for r in rows:
                     cells = src[j, r, q]
@@ -176,11 +198,10 @@
                             tap = (6 - i) * 7 + 6 - j if flip else i * 7 + j
                             term = cells * taps_ref[tap][None]
                             sums[p] = term if sums[p] is None else sums[p] + term
-            for p in range(H):
+            for p in live:
                 acc[p, q] = sums[p]
 
     own_rows = list(range(3, H + 3))
-    halo_rows = [0, 1, 2] + list(range(H + 3, H + 6))
     own_spread(xo, xs)
     conv(xs, own_rows, False, True)
     for p in range(H):
@@ -188,15 +209,15 @@
         cot[p, W:Wp] = jnp.zeros((Wp - W, C), F32)
     bsum[...] = jnp.zeros_like(bsum)
     chan[...] = jnp.zeros_like(chan)
-    halo_wait(x_halo, x_top, x_bot)
-    halo_spread(x_top, x_bot, xs)
-    conv(xs, halo_rows, False, False)
+    for a in range(2):
+        halo_arrive(*x_side, [a], [2 - a])
+        halo_spread(x_top, x_bot, xs, [a], [2 - a])
+    conv(xs, [1, 2, H + 3, H + 4], False, False)
 
     def rowsum(v):
         return jnp.sum(v, axis=0, keepdims=True)
 
-    @pl.loop(0, H)
-    def _(p):
+    def pointwise(p):
         conv_out = acc[p].reshape(Wp, C) + conv_bias_ref[...]
         dev = conv_out - jnp.mean(conv_out, axis=-1, keepdims=True)
         rstd = lax.rsqrt(jnp.mean(dev * dev, axis=-1, keepdims=True) + EPSILON)
@@ -245,15 +266,20 @@
         chan[3:4] += rowsum(gmix[p].astype(F32))
         chan[4:5] += rowsum(ocean * cot[p] * mixed)
 
-    g_halo = halo(gb, g_top, g_bot, 2)
-
-    @pl.when(t > 0)
-    def _():
-        g_halo[0].start()
-
-    @pl.when(t < n - 1)
-    def _():
-        g_halo[1].start()
+    @pl.loop(1, H - 1)
+    def _(p):
+        pointwise(p)
+
+    halo_start(*g_side, [1, 2], [1, 0])
+    halo_arrive(*x_side, [2], [0])
+    halo_spread(x_top, x_bot, xs, [2], [0])
+    conv(xs, [0, H + 5], False, False)
+
+    @pl.loop(0, 2)
+    def _(k):
+        pointwise(k * (H - 1))
+
+    halo_start(*g_side, [0], [2])
 
     flat = H * Wp
     tiles = part.shape[0] * part.shape[1] * part.shape[2] * part.shape[3]
@@ -285,14 +311,6 @@
     step1 = remote(part.at[1 - d], r1, send_sem.at[0], recv_sem.at[0], core)
     step1.start()
 
-    own_spread(gb, gs)
-    conv(gs, own_rows, True, True)
-
-    step1.wait()
-    r1[...] = (part[d].astype(F32) + r1[...].astype(F32)).astype(BF16)
-    step2 = remote(r1.at[1 - yy], r2, send_sem.at[1], recv_sem.at[1], beside)
-    step2.start()
-
     for j in range(7):
 
         def tap_terms(c, sums):
@@ -313,6 +331,11 @@
         for i in range(7):
             k = i * 7 + j
             sm[k // 32, k % 32 : k % 32 + 1] = rowsum(sums[i])
+    step1.wait()
+    r1[...] = (part[d].astype(F32) + r1[...].astype(F32)).astype(BF16)
+    step2 = remote(r1.at[1 - yy], r2, send_sem.at[1], recv_sem.at[1], beside)
+    step2.start()
+
     hidden_sum = rowsum(bsum[...])
     for k in range(HID // C):
         sm[1, 17 + k : 18 + k] = hidden_sum[:, k * C : k * C + C]
@@ -321,6 +344,10 @@
 
     small1 = remote(sm.at[1 - d], s1, send_sem.at[4], recv_sem.at[4], core)
     small1.start()
+
+    own_spread(gb, xs)
+    conv(xs, own_rows, True, True)
+
     step2.wait()
     r2[...] = (r1[yy].astype(F32) + r2[...].astype(F32)).astype(BF16)
     step3 = [
@@ -334,8 +361,8 @@
     small2 = remote(s2, s3, send_sem.at[5], recv_sem.at[5], beside)
     small2.start()
 
-    halo_wait(g_halo, g_top, g_bot)
-    halo_spread(g_top, g_bot, gs)
+    halo_arrive(*g_side, [1, 2], [1, 0])
+    halo_spread(g_top, g_bot, xs, [1, 2], [1, 0])
 
     for copy in step3:
         copy.wait()
@@ -359,7 +386,12 @@
     for copy in small3:
         copy.start()
 
-    conv(gs, halo_rows, True, False)
+    conv(xs, [0, 1, H + 4, H + 5], True, False)
+    halo_arrive(*g_side, [0], [2])
+    halo_spread(g_top, g_bot, xs, [0], [2])
+    conv(xs, [2, H + 3], True, False)
+    halo_sent(*x_side)
+    halo_sent(*g_side)
 
     for copy in step4:
         copy.wait()
@@ -381,7 +413,12 @@
     step6 = remote(whole.at[d], whole.at[d], send_sem.at[3], recv_sem.at[3], core)
     step6.start()
     small4.wait()
-    small_ref[...] = s6[...]
+    rows = s6[...].reshape(64, C)
+    for i in range(7):
+        kgrad_ref[i] = rows[i * 7 : i * 7 + 7]
+    for k in range(HID // C):
+        bgrad_ref[0:1, k * C : k * C + C] = rows[49 + k : 50 + k]
+    chan_ref[...] = rows[49 + HID // C : 54 + HID // C]
     step6.wait()
     for cb in range(HID // C):
         for rb in range(per):
@@ -430,7 +467,6 @@
         ((H, Wp, C), F32),
         ((Wp + 16, C), F32),
         ((7, H + 6, B, 8, C), F32),
-        ((7, H + 6, B, 8, C), F32),
         ((H, B, 8, C), F32),
         ((Wp, HID), F32),
         ((Wp, HID), F32),
@@ -456,28 +492,30 @@
         ((m, 32, C), F32),
         ((2, 32, C), F32),
     ]
-    output, input_grad, w_in_grad, w_out_grad, small = pl.pallas_call(
+    output, input_grad, w_in_grad, w_out_grad, kernel_grad, b_in_grad, channel = pl.pallas_call(
         functools.partial(block_kernel, n, scale),
         out_shape=(
             jax.ShapeDtypeStruct((H, W, C), BF16),
             jax.ShapeDtypeStruct((H, W, C), BF16),
             jax.ShapeDtypeStruct((C, HID), F32),
             jax.ShapeDtypeStruct((HID, C), F32),
-            jax.ShapeDtypeStruct((2, 32, C), F32),
+            jax.ShapeDtypeStruct((7, 7, C), F32),
+            jax.ShapeDtypeStruct((1, HID), F32),
+            jax.ShapeDtypeStruct((5, C), F32),
         ),
         in_specs=[vm] * 12,
-        out_specs=[vm] * 5,
+        out_specs=[vm] * 7,
         scratch_shapes=[pltpu.VMEM(shape, dtype) for shape, dtype in scratch]
         + [
-            pltpu.SemaphoreType.DMA((4,)),
-            pltpu.SemaphoreType.DMA((4,)),
+            pltpu.SemaphoreType.DMA((12,)),
+            pltpu.SemaphoreType.DMA((12,)),
             pltpu.SemaphoreType.DMA((7,)),
             pltpu.SemaphoreType.DMA((7,)),
             pltpu.SemaphoreType.DMA((3 * (m - 1),)),
             pltpu.SemaphoreType.DMA((3 * (m - 1),)),
         ],
         compiler_params=pltpu.CompilerParams(
-            collective_id=0, has_side_effects=True, vmem_limit_bytes=62 * 1024 * 1024
+            collective_id=0, has_side_effects=True, vmem_limit_bytes=60 * 1024 * 1024
         ),
     )(
         inputs[0],
@@ -493,15 +531,14 @@
         b_out[None],
         layer_scale[None],
     )
-    rows = small.reshape(64, C)
     return (
         output[None],
         input_grad[None],
-        rows[0:49].reshape(7, 7, C),
+        kernel_grad,
         w_in_grad,
         w_out_grad,
-        rows[49 : 49 + HID // C].reshape(HID),
-        rows[49 + HID // C : 54 + HID // C],
+        b_in_grad[0],
+        channel,
     )
 
 

time: 99.4 us -> 87.5 us (0.88)
  Pallas kernels: 86.1 us -> 74 us
    pallas_call x1, Pallas kernels: 86.1 us -> 74 us  [per_device(): pl.pallas_call(functools.partial(block_kernel, n, scale), out_shape=(jax....]
    unnamed x20 -> x25, local copies, waits for them, and re-layouts: 7.23 us -> 8.55 us
where the time goes in v2:
time: 87.5 us; the launch traced here: 87.2 us
  Pallas kernels  74 us (85%)
  local copies, waits for them, and re-layouts  12.4 us (14%)
    pallas_call x1, Pallas kernels, per_device(): pl.pallas_call(functools.partial(block_kernel, n, scale), out_shape=(jax....  74 us
    unnamed x25, local copies, waits for them, and re-layouts  8.55 us

profile of v2, /device:TPU:0, one launch (start us, length us, event | category | flops | bytes accessed | tf_op | source)
XLA Modules:
  0.0 87.2 jit_solution(8591749194519924423)
XLA Ops:
  0.6 0.0 copy-start.7
  0.6 0.7 copy-done.7
  1.3 0.0 copy-start.3
  1.4 0.0 copy-start.4
  1.4 0.9 %broadcast_in_dim.38 = f32[49,256]{1,0:T(8,128)S(1)} reshape(f32[7,7,256]{2,1,0:T(8,128)} %param.14) | data formatting | bytes 100352 | tf_op jit(solution)/shard_map/broadcast_in_dim | solution.py:461
  2.3 0.8 broadcast_in_dim.39.taps_ref
  3.1 1.0 %broadcast_in_dim.37.mask_ref = bf16[4,272,256]{2,1,0:T(8,128)(2,1)} broadcast(bf16[4,272]{1,0:T(4,128)(2,1)S(1)} %pad.5), dimensions={0,1} | broadcast | bytes 559232 | tf_op jit(solution)/shard_map/broadcast_in_dim | solution.py:458
  4.1 0.0 copy-done.3
  4.1 0.0 copy-done.4
  4.1 1.1 %copy_bitcast_fusion = (bf16[4,270,256]{2,1,0:T(8,128)(2,1)}, bf16[4,270,256]{2,1,0:T(8,128)(2,1)}) fusion(bf16[1,4,270,256]{3,1,2,0:T(4,128)(2,1)S(1)} %copy-done.3, bf16[1,4,270,256]{3,1,2,0:T(4,128)(2,1)S(1)} %copy-done.4), kind=kLoop, calls=%fused_computation | loop fusion | bytes 2211840 | tf_op jit(solution)/shard_map/squeeze | solution.py:522
  5.2 74.0 %shard_map.171 = (bf16[4,270,256]{2,1,0:T(8,128)(2,1)}, bf16[4,270,256]{2,1,0:T(8,128)(2,1)}, f32[256,1024]{1,0:T(8,128)}, f32[1024,256]{1,0:T(8,128)}, f32[7,7,...) custom-call(bf16[4,270,256]{2,1,0:T(8,128)(2,1)} %get-tuple-element.29.x_ref, ...), custom_call_target="tpu_custom_call" | custom-call | tf_op jit(solution)/shard_map/pallas_call | solution.py:495
  79.3 0.0 copy-start.2
  79.3 0.0 copy-start.1
  79.3 2.3 %copy.21 = bf16[1,4,270,256]{3,1,2,0:T(4,128)(2,1)} copy(bf16[1,4,270,256]{3,2,1,0:T(8,128)(2,1)} %bitcast.14) | data formatting | bytes 1105920
  81.6 0.0 copy-done.2
  81.6 0.0 copy-start.5
  81.6 1.1 %copy.22 = bf16[1,4,270,256]{3,1,2,0:T(4,128)(2,1)} copy(bf16[1,4,270,256]{3,2,1,0:T(8,128)(2,1)S(1)} %bitcast.13) | data formatting | bytes 1105920
  82.6 0.0 copy-done.5
  82.7 0.6 copy.30
  83.3 0.0 copy-done.1
  83.3 0.0 copy-start
  83.3 1.0 %copy.31 = f32[256,1024]{1,0:T(8,128)} copy(f32[256,1024]{1,0:T(8,128)S(1)} %copy-done.1) | data formatting | bytes 2097152
  84.2 0.6 copy-done
  84.9 0.0 copy-start.8
  84.9 1.0 %copy.32 = f32[1024,256]{1,0:T(8,128)} copy(f32[1024,256]{1,0:T(8,128)S(1)} %copy-done) | data formatting | bytes 2097152
  85.9 0.0 copy-done.8
  85.9 0.0 copy-start.6
  85.9 0.6 copy.33
  86.5 0.1 copy-done.6
  86.6 0.6 copy.34
  (2 shorter events, 0.0 us)
Async XLA Ops:
  0.6 0.7 copy-start.7
  1.3 2.7 %copy-start.3 = (bf16[1,4,270,256]{3,1,2,0:T(4,128)(2,1)S(1)}, bf16[1,4,270,256]{3,1,2,0:T(4,128)(2,1)}, u32[]{:S(2)}) copy-start(bf16[1,4,270,256]{3,1,2,0:T(4,128)(2,1)} %param.23) | copy-start | bytes 1658884
  1.4 2.7 %copy-start.4 = (bf16[1,4,270,256]{3,1,2,0:T(4,128)(2,1)S(1)}, bf16[1,4,270,256]{3,1,2,0:T(4,128)(2,1)}, u32[]{:S(2)}) copy-start(bf16[1,4,270,256]{3,1,2,0:T(4,128)(2,1)} %param.12) | copy-start | bytes 1658884
  79.3 2.3 %copy-start.2 = (bf16[4,270,256]{2,1,0:T(8,128)(2,1)S(1)}, bf16[4,270,256]{2,1,0:T(8,128)(2,1)}, u32[]{:S(2)}) copy-start(bf16[4,270,256]{2,1,0:T(8,128)(2,1)} %get-tuple-element.15) | copy-start | bytes 1658884
  79.3 4.0 %copy-start.1 = (f32[256,1024]{1,0:T(8,128)S(1)}, f32[256,1024]{1,0:T(8,128)}, u32[]{:S(2)}) copy-start(f32[256,1024]{1,0:T(8,128)} %get-tuple-element.40) | copy-start | bytes 3145732
  81.6 1.1 %copy-start.5 = (f32[7,7,256]{2,1,0:T(8,128)S(1)}, f32[7,7,256]{2,1,0:T(8,128)}, u32[]{:S(2)}) copy-start(f32[7,7,256]{2,1,0:T(8,128)} %get-tuple-element.39) | copy-start | bytes 150532
  83.3 1.6 %copy-start = (f32[1024,256]{1,0:T(8,128)S(1)}, f32[1024,256]{1,0:T(8,128)}, u32[]{:S(2)}) copy-start(f32[1024,256]{1,0:T(8,128)} %get-tuple-element.41) | copy-start | bytes 3145732
  84.9 1.0 %copy-start.8 = (f32[1,1024]{1,0:T(1,128)S(1)}, f32[1,1024]{1,0:T(1,128)}, u32[]{:S(2)}) copy-start(f32[1,1024]{1,0:T(1,128)} %get-tuple-element.19) | copy-start | bytes 12292
  85.9 0.7 copy-start.6
